TPU v7x, 32 devices: a whole 2x2x4 slice. The times are simulated.
32 devices in a mesh: seg: 4 (over y, x), op: 8 (over z, core).
Axes of the slice: x: 2, y: 2, z: 4, core: 2. Of those that a mesh axis runs over, the one named last changes fastest.
Arguments:
- theta: bfloat16 [4, 8, 512, 512], P('seg', 'op'), may hold values from -21 to 21
- left_edge: bfloat16 [8, 512, 512], P('op'), may hold values from -1 to 4
- transfer: bfloat16 [4, 8, 512, 512], P('seg', 'op'), may hold values from -1 to 2
- right_env: bfloat16 [4, 8, 512, 512], P('seg', 'op'), may hold values from -1 to 4
- coupling: bfloat16 [4, 8, 512, 512], P('seg', 'op'), may hold values from -0.25 to 0.25
- left_sizes: int32 [8], P('op'), may hold values from 1 to 512, 3072 in all
- right_sizes: int32 [8], P('op'), may hold values from 1 to 512, 3072 in all
Outputs:
- theta_out: float32 [4, 8, 512, 512], P('seg', 'op')
- left_env: bfloat16 [4, 8, 512, 512], P('seg', 'op')
- energy: float32 [4], P('seg')
- first_energy: float32 [4], P('seg')
All inputs are finite; a program needn't handle non-finite values. No bound on the sum of `left_sizes` or of `right_sizes` on one device may be relied on, other than what follows from the above.
Results may differ from a plain program's by a relative error of at most 0.0085.
Values may be sent and summed in bfloat16 or wider, within the bound.
A program may use at most 128 MiB of HBM per device.

v0:
```python
import jax
import jax.numpy as jnp
from jax import lax
from jax.sharding import PartitionSpec as P

DAVIDSON = 4


epsilon = 1e-06


def carried_in(value, axis, join, neutral):
    count, mine = (lax.axis_size(axis), lax.axis_index(axis))
    pieces = lax.all_gather(value, axis)
    so_far = jnp.full_like(value, 0) + jnp.asarray(neutral, value.dtype)

    def lap(position, so_far):
        longer = join(so_far, pieces[position])
        return jnp.where(position < mine, longer, so_far)

    return lax.fori_loop(0, count - 1, lap, so_far)


def from_behind(block, axis, distance):
    devices = range(lax.axis_size(axis))
    route = [(i - distance, i) for i in devices if i - distance in devices]
    return lax.ppermute(block, axis, route)


def symmetric(block):
    return 0.5 * (block + jnp.swapaxes(block, -1, -2))


def compose(earlier, later):
    return jnp.einsum("kij,kjl->kil", earlier, later, precision=lax.Precision.HIGHEST)


def on_device(theta, left_edge, transfer, right_env, coupling, left_sizes, right_sizes):
    sectors_here = theta.shape[1]
    block_size = theta.shape[3]
    highest = lax.Precision.HIGHEST
    transfers = transfer[0].astype(jnp.float32)
    identity = jnp.broadcast_to(
        jnp.eye(block_size, dtype=jnp.float32), (sectors_here, block_size, block_size)
    )
    prefix = carried_in(transfers, "seg", compose, identity)
    edge_sym = symmetric(left_edge.astype(jnp.float32))
    left_block = jnp.einsum("kji,kjl->kil", prefix, edge_sym, precision=highest)
    left_block = jnp.einsum("kij,kjl->kil", left_block, prefix, precision=highest).astype(
        jnp.bfloat16
    )
    right_block = symmetric(right_env[0].astype(jnp.float32)).astype(jnp.bfloat16)
    coupling_blk = coupling[0]
    row_index = lax.broadcasted_iota(jnp.int32, (sectors_here, block_size, block_size), 1)
    col_index = lax.broadcasted_iota(jnp.int32, (sectors_here, block_size, block_size), 2)
    live_mask = (
        (row_index < left_sizes[:, None, None]) & (col_index < right_sizes[:, None, None])
    ).astype(jnp.float32)

    def apply_field(field):
        middle = jnp.einsum(
            "kij,kjl->kil", left_block, field, preferred_element_type=jnp.float32
        ).astype(jnp.bfloat16)
        diagonal_term = jnp.einsum(
            "kij,kjl->kil", middle, right_block, preferred_element_type=jnp.float32
        )
        received_low = from_behind(field[-1], "op", 1)
        previous = jnp.concatenate([received_low[None], field[:-1]], 0)
        lifted = jnp.einsum("kji,kjl->kil", coupling_blk, field, preferred_element_type=jnp.float32)
        received_up = from_behind(lifted[0], "op", -1)
        upper_part = jnp.concatenate([lifted[1:], received_up[None]], 0)
        lower_term = jnp.einsum(
            "kij,kjl->kil", coupling_blk, previous, preferred_element_type=jnp.float32
        )
        return live_mask * (diagonal_term + lower_term + upper_part)

    start = live_mask * theta[0].astype(jnp.float32)
    start_total = lax.psum(jnp.sum(start * start), "op")
    vector = start / jnp.sqrt(start_total + epsilon)
    image = apply_field(vector.astype(jnp.bfloat16))
    energy = lax.psum(jnp.sum(vector * image), "op")
    first_value = energy
    for sweep_step in range(DAVIDSON):
        residual = image - energy * vector
        correction = residual.astype(jnp.bfloat16)
        corr_wide = correction.astype(jnp.float32)
        corr_norm, cross_term = lax.psum(
            (jnp.sum(corr_wide * corr_wide), jnp.sum(image * corr_wide)), "op"
        )
        applied = apply_field(correction)
        curv_term = lax.psum(jnp.sum(corr_wide * applied), "op")
        scale_norm = jnp.sqrt(corr_norm + epsilon)
        offdiag = cross_term / scale_norm
        diag_value = curv_term / (corr_norm + epsilon)
        half_gap = (diag_value - energy) / 2
        lowest = (energy + diag_value) / 2 - jnp.sqrt(half_gap * half_gap + offdiag * offdiag)
        rotation = lowest - energy
        radius = jnp.sqrt(offdiag * offdiag + rotation * rotation + epsilon)
        vector = (offdiag * vector + rotation * corr_wide / scale_norm) / radius
        image = (offdiag * image + rotation * applied / scale_norm) / radius
        energy = lowest
    return (
        vector[None],
        left_block[None],
        jnp.reshape(energy, (1,)),
        jnp.reshape(first_value, (1,)),
    )


def solution(mesh):
    placed = (
        P("seg", "op", None, None),
        P("op", None, None),
        P("seg", "op", None, None),
        P("seg", "op", None, None),
        P("seg", "op", None, None),
        P("op"),
        P("op"),
    )
    return jax.shard_map(
        on_device,
        mesh=mesh,
        in_specs=placed,
        out_specs=(P("seg", "op", None, None), P("seg", "op", None, None), P("seg"), P("seg")),
        check_vma=False,
    )
```

profile of v0, /device:TPU:6, one launch (start us, length us, event | category | flops | bytes accessed | tf_op | source)
XLA Modules:
  0.0 260.4 jit_solution(6043262322751508550)
XLA Ops:
  12.8 17.2 %psum.98 = f32[]{:T(128)} all-reduce(f32[]{:T(128)} %fusion.30), channel_id=1, replica_groups=mesh['seg'=4,'op'=8] {'op'}, use_global_device_ids=true, to_apply=%region_3.4 | all-reduce | flops 1 | bytes 8 | tf_op jit(solution)/shard_map/psum | solution.py:78
  43.0 19.9 %all-gather.2.cloned.1.call-done = f32[4,1,512,512]{3,2,1,0:T(8,128)} async-done(((f32[1,1,512,512]{3,2,1,0:T(8,128)}), f32[4,1,512,512]{3,2,1,0:T(8,128)}) %all-gather.2.cloned.1.call-update) | async-done | bytes 4194320 | tf_op jit(solution)/shard_map/all_gather | solution.py:14
  62.9 9.5 %while.13 = (s32[]{:T(128)}, f32[1,512,512]{1,2,0:T(8,128)S(1)}, s32[]{:T(128)}, f32[4,1,512,512]{3,2,1,0:T(8,128)}, s32[]{:T(128)}) while((s32[]{:T(128)}, f32[1,512,512]{1,2,0:T(8,128)S(1)}, s32[]{:T(128)}, f32[4,1,512,512]{3,2,1,0:T(8,128)}, s32[]{:T(128)}) %tuple.47), condition=%wide.region_1.2_spmd, body=%wide.region_0.1_spmd.sunk | while | flops 1610874880 | bytes 6292039 | solution.py:21
  62.9 3.1 %fusion.121 = f32[1,512,512]{1,2,0:T(8,128)S(1)} fusion(f32[1,512,512]{1,2,0:T(8,128)S(1)} %copy.58, f32[4,1,512,512]{3,2,1,0:T(8,128)} %get-tuple-element.164, s32[]{:T(128)} %get-tuple-element.156, pred[]{:T(512)S(6)} %lt.241), kind=kOutput, calls=%fused_computation.1.clone.1 | convolution fusion | flops 1610874880 | bytes 4194817 | tf_op jit(solution)/shard_map/while/body/eval_jaxpr/kij,kjl->kil/dot_general | solution.py:35
  66.1 3.1 %fusion.121 = f32[1,512,512]{1,2,0:T(8,128)S(1)} fusion(f32[1,512,512]{1,2,0:T(8,128)S(1)} %copy.58, f32[4,1,512,512]{3,2,1,0:T(8,128)} %get-tuple-element.164, s32[]{:T(128)} %get-tuple-element.156, pred[]{:T(512)S(6)} %lt.241), kind=kOutput, calls=%fused_computation.1.clone.1 | convolution fusion | flops 1610874880 | bytes 4194817 | tf_op jit(solution)/shard_map/while/body/eval_jaxpr/kij,kjl->kil/dot_general | solution.py:35
  69.3 3.1 %fusion.121 = f32[1,512,512]{1,2,0:T(8,128)S(1)} fusion(f32[1,512,512]{1,2,0:T(8,128)S(1)} %copy.58, f32[4,1,512,512]{3,2,1,0:T(8,128)} %get-tuple-element.164, s32[]{:T(128)} %get-tuple-element.156, pred[]{:T(512)S(6)} %lt.241), kind=kOutput, calls=%fused_computation.1.clone.1 | convolution fusion | flops 1610874880 | bytes 4194817 | tf_op jit(solution)/shard_map/while/body/eval_jaxpr/kij,kjl->kil/dot_general | solution.py:35
  72.4 3.1 %fusion.57 = f32[512,512]{1,0:T(8,128)S(1)} fusion(f32[1,512,512]{2,1,0:T(8,128)} %copy.25, f32[1,512,512]{1,2,0:T(8,128)S(1)} %get-tuple-element.83, bf16[1,512,512]{1,2,0:T(8,128)(2,1)S(1)} %copy.24), kind=kOutput, calls=%fused_computation.93 | convolution fusion | flops 1611399168 | bytes 3670016 | tf_op jit(solution)/shard_map/kji,kjl->kil/dot_general | solution.py:48
  77.4 3.1 %fusion.20 = f32[512,512]{1,0:T(8,128)} fusion(bf16[512,512]{1,0:T(8,128)(2,1)} %fusion.68, bf16[512,512]{1,0:T(8,128)(2,1)S(1)} %convolution_convert_fusion.5, bf16[512,512]{1,0:T(8,128)(2,1)} %fusion.89), kind=kOutput, calls=%fused_computation.55 | convolution fusion | flops 537133056 | bytes 2621440 | tf_op jit(solution)/shard_map/kij,kjl->kil/dot_general | solution.py:64
  83.5 17.0 %psum.99 = f32[]{:T(128)} all-reduce(f32[]{:T(128)} %get-tuple-element.121), channel_id=1, replica_groups=mesh['seg'=4,'op'=8] {'op'}, use_global_device_ids=true, to_apply=%region_5.6 | all-reduce | flops 1 | bytes 8 | tf_op jit(solution)/shard_map/psum | solution.py:81
  104.2 3.8 %collective-permute-start.2 = (bf16[512,512]{1,0:T(8,128)(2,1)S(1)}, bf16[512,512]{1,0:T(8,128)(2,1)}, u32[]{:S(2)}, u32[]{:S(2)}) collective-permute-start(bf16[512,512]{1,0:T(8,128)(2,1)S(1)} %subtract_convert_fusion.3), channel_id=1, source_target_pairs={{0,1},{1,2},{2,3},{3,4},{4,5},{5,6},{6,7},{8,9},{9,10},{10,11},{11... | collective-permute-start | bytes 1572872 | tf_op jit(solution)/shard_map/ppermute | solution.py:27
  110.8 3.9 %fusion.34 = (f32[]{:T(128)}, f32[]{:T(128)}, f32[]{:T(128)}, f32[512,512]{1,0:T(8,128)}) fusion(bf16[512,512]{1,0:T(8,128)(2,1)S(1)} %subtract_convert_fusion.3, f32[512,512]{1,0:T(8,128)S(1)} %get-tuple-element.122, f32[512,512]{1,0:T(8,128)} %collective-permute-done.3, f32[512,512]{1,0:T(8,128)} %fusion.21, bf16[512,512]{1,0:T(8,128)(2,1)} %collective-permute-done.2, ...), kind=kOutput, calls=%fused_computation.69 | convolution fusion | flops 271843328 | bytes 5767188 | tf_op jit(solution)/shard_map/kij,kjl->kil/dot_general | solution.py:72
  114.6 20.1 %all-reduce.3 = (f32[]{:T(128)}, f32[]{:T(128)}, f32[]{:T(128)}) all-reduce(f32[]{:T(128)} %get-tuple-element.94, f32[]{:T(128)} %get-tuple-element.93, f32[]{:T(128)} %get-tuple-element.92), channel_id=1, replica_groups=mesh['seg'=4,'op'=8] {'op'}, use_global_device_ids=true, to_apply=%region_7.8 | all-reduce | flops 3 | bytes 24 | tf_op jit(solution)/shard_map/psum | solution.py:87
  143.6 3.9 %collective-permute-start.4 = (bf16[512,512]{1,0:T(8,128)(2,1)S(1)}, bf16[512,512]{1,0:T(8,128)(2,1)}, u32[]{:S(2)}, u32[]{:S(2)}) collective-permute-start(bf16[512,512]{1,0:T(8,128)(2,1)S(1)} %get-tuple-element.119), channel_id=1, source_target_pairs={{0,1},{1,2},{2,3},{3,4},{4,5},{5,6},{6,7},{8,9},{9,10},{10,11},{11... | collective-permute-start | bytes 1572872 | tf_op jit(solution)/shard_map/ppermute | solution.py:27
  150.4 3.9 %fusion.40 = (f32[]{:T(128)}, f32[]{:T(128)}, f32[]{:T(128)}, f32[512,512]{1,0:T(8,128)}) fusion(bf16[512,512]{1,0:T(8,128)(2,1)S(1)} %get-tuple-element.119, f32[512,512]{1,0:T(8,128)S(1)} %get-tuple-element.120, f32[512,512]{1,0:T(8,128)} %collective-permute-done.5, f32[512,512]{1,0:T(8,128)} %fusion.22, bf16[512,512]{1,0:T(8,128)(2,1)} %collective-permute-done.4, ...), kind=kOutput, calls=%fused_computation.75 | convolution fusion | flops 271843328 | bytes 5767188 | tf_op jit(solution)/shard_map/kij,kjl->kil/dot_general | solution.py:72
  154.2 19.0 %all-reduce.2 = (f32[]{:T(128)}, f32[]{:T(128)}, f32[]{:T(128)}) all-reduce(f32[]{:T(128)} %get-tuple-element.91, f32[]{:T(128)} %get-tuple-element.90, f32[]{:T(128)} %get-tuple-element.89), channel_id=1, replica_groups=mesh['seg'=4,'op'=8] {'op'}, use_global_device_ids=true, to_apply=%region_13.14 | all-reduce | flops 3 | bytes 24 | tf_op jit(solution)/shard_map/psum | solution.py:87
  175.2 3.6 %subtract_convert_fusion.1 = (bf16[512,512]{1,0:T(8,128)(2,1)S(1)}, f32[512,512]{1,0:T(8,128)S(1)}, f32[512,512]{1,0:T(8,128)}) fusion(f32[]{:T(128)S(6)} %sub.58, f32[]{:T(128)S(6)} %sqrt.45, f32[]{:T(128)S(6)} %sqrt.43, bf16[512,512]{1,0:T(8,128)(2,1)} %copy-done.5, f32[]{:T(128)S(6)} %sub.59, f32[]{:T(128)S(6)} %sqrt.42, f32[]{:T(128)S(6)} %sqrt.40, ...), kind=kLoop, calls=%fused_computation.101 | loop fusion | flops 6815744 | bytes 6291504 | tf_op jit(solution)/shard_map/convert_element_type | solution.py:85
  181.6 3.8 %collective-permute-start.6 = (bf16[512,512]{1,0:T(8,128)(2,1)S(1)}, bf16[512,512]{1,0:T(8,128)(2,1)}, u32[]{:S(2)}, u32[]{:S(2)}) collective-permute-start(bf16[512,512]{1,0:T(8,128)(2,1)S(1)} %get-tuple-element.116), channel_id=1, source_target_pairs={{0,1},{1,2},{2,3},{3,4},{4,5},{5,6},{6,7},{8,9},{9,10},{10,11},{11... | collective-permute-start | bytes 1572872 | tf_op jit(solution)/shard_map/ppermute | solution.py:27
  188.4 3.9 %fusion.46 = (f32[]{:T(128)}, f32[]{:T(128)}, f32[]{:T(128)}, f32[512,512]{1,0:T(8,128)}) fusion(bf16[512,512]{1,0:T(8,128)(2,1)S(1)} %get-tuple-element.116, f32[512,512]{1,0:T(8,128)S(1)} %copy-done.2, f32[512,512]{1,0:T(8,128)} %collective-permute-done.7, f32[512,512]{1,0:T(8,128)} %fusion.23, bf16[512,512]{1,0:T(8,128)(2,1)} %collective-permute-done.6, ...), kind=kOutput, calls=%fused_computation.81 | convolution fusion | flops 271843328 | bytes 5767188 | tf_op jit(solution)/shard_map/kij,kjl->kil/dot_general | solution.py:72
  192.2 19.0 %all-reduce.1 = (f32[]{:T(128)}, f32[]{:T(128)}, f32[]{:T(128)}) all-reduce(f32[]{:T(128)} %get-tuple-element.88, f32[]{:T(128)} %get-tuple-element.87, f32[]{:T(128)} %get-tuple-element.86), channel_id=1, replica_groups=mesh['seg'=4,'op'=8] {'op'}, use_global_device_ids=true, to_apply=%region_19.20 | all-reduce | flops 3 | bytes 24 | tf_op jit(solution)/shard_map/psum | solution.py:87
  213.2 3.3 %fusion.51 = (f32[]{:T(128)}, f32[]{:T(128)}, bf16[512,512]{1,0:T(8,128)(2,1)}) fusion(f32[]{:T(128)S(6)} %sqrt.48, f32[]{:T(128)S(6)} %sqrt.46, bf16[512,512]{1,0:T(8,128)(2,1)S(1)} %get-tuple-element.116, f32[]{:T(128)S(6)} %sub.63, f32[512,512]{1,0:T(8,128)S(1)} %get-tuple-element.117, f32[]{:T(128)S(6)} %div.177, f32[]{:T(128)S(6)} %sub.62, ...), kind=kLoop, calls=%fused_computation.86 | loop fusion | flops 4980734 | bytes 4194332 | tf_op jit(solution)/shard_map/reduce_sum | solution.py:88
  219.3 3.9 %collective-permute-start.8 = (bf16[512,512]{1,0:T(8,128)(2,1)}, bf16[512,512]{1,0:T(8,128)(2,1)}, u32[]{:S(2)}, u32[]{:S(2)}) collective-permute-start(bf16[512,512]{1,0:T(8,128)(2,1)} %get-tuple-element.115), channel_id=1, source_target_pairs={{0,1},{1,2},{2,3},{3,4},{4,5},{5,6},{6,7},{8,9},{9,10},{10,11},{11... | collective-permute-start | bytes 1572872 | tf_op jit(solution)/shard_map/ppermute | solution.py:27
  223.2 3.0 %fusion.24 = f32[512,512]{1,0:T(8,128)} fusion(bf16[512,512]{1,0:T(8,128)(2,1)} %fusion.68, bf16[512,512]{1,0:T(8,128)(2,1)} %copy-done.7, bf16[512,512]{1,0:T(8,128)(2,1)} %get-tuple-element.115), kind=kOutput, calls=%fused_computation.59 | convolution fusion | flops 537133056 | bytes 2621440 | tf_op jit(solution)/shard_map/kij,kjl->kil/dot_general | solution.py:64
  226.2 3.1 %fusion.67 = f32[]{:T(128)} fusion(f32[512,512]{1,0:T(8,128)} %collective-permute-done.9, f32[512,512]{1,0:T(8,128)} %fusion.24, bf16[512,512]{1,0:T(8,128)(2,1)} %collective-permute-done.8, bf16[512,512]{1,0:T(8,128)(2,1)} %get-tuple-element.115, bf16[1,1,512,512]{3,2,1,0:T(8,128)(2,1)S(1)} %copy-done, s32[]{:T(128)} %bitcast.214, s32[]{:T(128)} %bitcast.203), kind=kOutput, calls=%fused_computation.116 | convolution fusion | flops 270794752 | bytes 3670028 | tf_op jit(solution)/shard_map/kij,kjl->kil/dot_general | solution.py:72
  229.3 18.7 %all-reduce = (f32[]{:T(128)}, f32[]{:T(128)}, f32[]{:T(128)}) all-reduce(f32[]{:T(128)} %get-tuple-element.85, f32[]{:T(128)} %get-tuple-element.84, f32[]{:T(128)} %fusion.67), channel_id=1, replica_groups=mesh['seg'=4,'op'=8] {'op'}, use_global_device_ids=true, to_apply=%region_25.26 | all-reduce | flops 3 | bytes 24 | tf_op jit(solution)/shard_map/psum | solution.py:87
  (61 shorter events, 46.8 us)
Async XLA Ops:
  7.2 27.8 %copy-start = (bf16[1,1,512,512]{3,2,1,0:T(8,128)(2,1)S(1)}, bf16[1,1,512,512]{3,2,1,0:T(8,128)(2,1)}, u32[]{:S(2)}) copy-start(bf16[1,1,512,512]{3,2,1,0:T(8,128)(2,1)} %param.13) | copy-start | bytes 1572868
  7.2 27.8 %copy-start.1 = (bf16[1,1,512,512]{3,2,1,0:T(8,128)(2,1)S(1)}, bf16[1,1,512,512]{3,2,1,0:T(8,128)(2,1)}, u32[]{:S(2)}) copy-start(bf16[1,1,512,512]{3,2,1,0:T(8,128)(2,1)} %param.9) | copy-start | bytes 1572868
  7.2 55.7 %all-gather.2.cloned.1.call-start = ((), (), s32[]{:S(2)}) async-start(), calls=%async_computation | async-start | bytes 5242880 | tf_op jit(solution)/shard_map/all_gather | solution.py:14
  9.5 28.2 %copy-start.8 = (bf16[1,512,512]{2,1,0:T(8,128)(2,1)S(1)}, bf16[1,512,512]{2,1,0:T(8,128)(2,1)}, u32[]{:S(2)}) copy-start(bf16[1,512,512]{2,1,0:T(8,128)(2,1)} %param.10) | copy-start | bytes 1572868
  32.9 47.6 %collective-permute-start = (bf16[512,512]{1,0:T(8,128)(2,1)}, bf16[512,512]{1,0:T(8,128)(2,1)}, u32[]{:S(2)}, u32[]{:S(2)}) collective-permute-start(bf16[512,512]{1,0:T(8,128)(2,1)} %fusion.89), channel_id=1, source_target_pairs={{0,1},{1,2},{2,3},{3,4},{4,5},{5,6},{6,7},{8,9},{9,10},{10,11},{11... | collective-permute-start | bytes 1572872 | tf_op jit(solution)/shard_map/ppermute | solution.py:27
  35.0 4.2 %copy-start.6 = (bf16[1,1,512,512]{3,2,1,0:T(8,128)(2,1)S(1)}, bf16[1,1,512,512]{3,2,1,0:T(8,128)(2,1)}, u32[]{:S(2)}) copy-start(bf16[1,1,512,512]{3,2,1,0:T(8,128)(2,1)} %param.12) | copy-start | bytes 1572868
  36.5 44.1 %collective-permute-start.1 = (f32[512,512]{1,0:T(8,128)}, f32[512,512]{1,0:T(8,128)}, u32[]{:S(2)}, u32[]{:S(2)}) collective-permute-start(f32[512,512]{1,0:T(8,128)} %convolution_bitcast_fusion.10), channel_id=1, source_target_pairs={{1,0},{2,1},{3,2},{4,3},{5,4},{6,5},{7,6},{9,8},{10,9},{11,10},{12... | collective-permute-start | bytes 3145736 | tf_op jit(solution)/shard_map/ppermute | solution.py:27
  77.4 30.6 %copy-start.7 = (bf16[512,512]{1,0:T(8,128)(2,1)}, bf16[512,512]{1,0:T(8,128)(2,1)S(1)}, u32[]{:S(2)}) copy-start(bf16[512,512]{1,0:T(8,128)(2,1)S(1)} %convolution_convert_fusion.5) | copy-start | bytes 1572868
  83.5 31.1 %copy-start.4 = (f32[512,512]{1,0:T(8,128)}, f32[512,512]{1,0:T(8,128)S(1)}, u32[]{:S(2)}) copy-start(f32[512,512]{1,0:T(8,128)S(1)} %get-tuple-element.122) | copy-start | bytes 3145732
  102.9 7.9 %collective-permute-start.3 = (f32[512,512]{1,0:T(8,128)}, f32[512,512]{1,0:T(8,128)}, u32[]{:S(2)}, u32[]{:S(2)}) collective-permute-start(f32[512,512]{1,0:T(8,128)} %convolution_bitcast_fusion.9), channel_id=1, source_target_pairs={{1,0},{2,1},{3,2},{4,3},{5,4},{6,5},{7,6},{9,8},{10,9},{11,10},{12... | collective-permute-start | bytes 3145736 | tf_op jit(solution)/shard_map/ppermute | solution.py:27
  104.2 6.6 %collective-permute-start.2 = (bf16[512,512]{1,0:T(8,128)(2,1)S(1)}, bf16[512,512]{1,0:T(8,128)(2,1)}, u32[]{:S(2)}, u32[]{:S(2)}) collective-permute-start(bf16[512,512]{1,0:T(8,128)(2,1)S(1)} %subtract_convert_fusion.3), channel_id=1, source_target_pairs={{0,1},{1,2},{2,3},{3,4},{4,5},{5,6},{6,7},{8,9},{9,10},{10,11},{11... | collective-permute-start | bytes 1572872 | tf_op jit(solution)/shard_map/ppermute | solution.py:27
  140.8 13.4 %copy-start.3 = (f32[512,512]{1,0:T(8,128)}, f32[512,512]{1,0:T(8,128)S(1)}, u32[]{:S(2)}) copy-start(f32[512,512]{1,0:T(8,128)S(1)} %get-tuple-element.120) | copy-start | bytes 3145732
  140.8 13.4 %copy-start.5 = (bf16[512,512]{1,0:T(8,128)(2,1)}, bf16[512,512]{1,0:T(8,128)(2,1)S(1)}, u32[]{:S(2)}) copy-start(bf16[512,512]{1,0:T(8,128)(2,1)S(1)} %get-tuple-element.119) | copy-start | bytes 1572868
  142.3 8.0 %collective-permute-start.5 = (f32[512,512]{1,0:T(8,128)}, f32[512,512]{1,0:T(8,128)}, u32[]{:S(2)}, u32[]{:S(2)}) collective-permute-start(f32[512,512]{1,0:T(8,128)} %convolution_bitcast_fusion.8), channel_id=1, source_target_pairs={{1,0},{2,1},{3,2},{4,3},{5,4},{6,5},{7,6},{9,8},{10,9},{11,10},{12... | collective-permute-start | bytes 3145736 | tf_op jit(solution)/shard_map/ppermute | solution.py:27
  143.6 6.8 %collective-permute-start.4 = (bf16[512,512]{1,0:T(8,128)(2,1)S(1)}, bf16[512,512]{1,0:T(8,128)(2,1)}, u32[]{:S(2)}, u32[]{:S(2)}) collective-permute-start(bf16[512,512]{1,0:T(8,128)(2,1)S(1)} %get-tuple-element.119), channel_id=1, source_target_pairs={{0,1},{1,2},{2,3},{3,4},{4,5},{5,6},{6,7},{8,9},{9,10},{10,11},{11... | collective-permute-start | bytes 1572872 | tf_op jit(solution)/shard_map/ppermute | solution.py:27
  178.8 9.5 %copy-start.2 = (f32[512,512]{1,0:T(8,128)S(1)}, f32[512,512]{1,0:T(8,128)}, u32[]{:S(2)}) copy-start(f32[512,512]{1,0:T(8,128)} %get-tuple-element.118) | copy-start | bytes 3145732
  180.3 8.1 %collective-permute-start.7 = (f32[512,512]{1,0:T(8,128)}, f32[512,512]{1,0:T(8,128)}, u32[]{:S(2)}, u32[]{:S(2)}) collective-permute-start(f32[512,512]{1,0:T(8,128)} %convolution_bitcast_fusion.7), channel_id=1, source_target_pairs={{1,0},{2,1},{3,2},{4,3},{5,4},{6,5},{7,6},{9,8},{10,9},{11,10},{12... | collective-permute-start | bytes 3145736 | tf_op jit(solution)/shard_map/ppermute | solution.py:27
  181.6 6.8 %collective-permute-start.6 = (bf16[512,512]{1,0:T(8,128)(2,1)S(1)}, bf16[512,512]{1,0:T(8,128)(2,1)}, u32[]{:S(2)}, u32[]{:S(2)}) collective-permute-start(bf16[512,512]{1,0:T(8,128)(2,1)S(1)} %get-tuple-element.116), channel_id=1, source_target_pairs={{0,1},{1,2},{2,3},{3,4},{4,5},{5,6},{6,7},{8,9},{9,10},{10,11},{11... | collective-permute-start | bytes 1572872 | tf_op jit(solution)/shard_map/ppermute | solution.py:27
  218.0 8.2 %collective-permute-start.9 = (f32[512,512]{1,0:T(8,128)S(1)}, f32[512,512]{1,0:T(8,128)}, u32[]{:S(2)}, u32[]{:S(2)}) collective-permute-start(f32[512,512]{1,0:T(8,128)S(1)} %convolution_bitcast_fusion.6), channel_id=1, source_target_pairs={{1,0},{2,1},{3,2},{4,3},{5,4},{6,5},{7,6},{9,8},{10,9},{11,10},{12... | collective-permute-start | bytes 3145736 | tf_op jit(solution)/shard_map/ppermute | solution.py:27
  219.3 6.9 %collective-permute-start.8 = (bf16[512,512]{1,0:T(8,128)(2,1)}, bf16[512,512]{1,0:T(8,128)(2,1)}, u32[]{:S(2)}, u32[]{:S(2)}) collective-permute-start(bf16[512,512]{1,0:T(8,128)(2,1)} %get-tuple-element.115), channel_id=1, source_target_pairs={{0,1},{1,2},{2,3},{3,4},{4,5},{5,6},{6,7},{8,9},{9,10},{10,11},{11... | collective-permute-start | bytes 1572872 | tf_op jit(solution)/shard_map/ppermute | solution.py:27
Sparse Core Ops, SparseCore 0:
  9.9 52.9 all-gather.1
where the time goes:
time: 264 us; the launch traced here: 260 us
  blocking collectives  111 us (42%)
  matrix products  54 us (20%)
  between operations  27.3 us (10%)
  starting transfers between devices  23.9 us (9%)
  other arithmetic  21.3 us (8%)
  waiting for transfers between devices  19.9 us (8%)
  local copies, waits for them, and re-layouts  3 us (1%)
    psum x4, blocking collectives, on_device(): lax.psum((jnp.sum(corr_wide * corr_wide), jnp.sum(image * corr_wide)), 'op')  76.8 us
    ppermute x10, starting transfers between devices, from_behind(): return lax.ppermute(block, axis, route)  23.9 us
    all_gather x1, waiting for transfers between devices, carried_in(): pieces = lax.all_gather(value, axis)  19.9 us
    dot_general x5, matrix products, apply_field(): jnp.einsum('kij,kjl->kil', coupling_blk, previous, preferred_element_type...  17.7 us
    psum x1, blocking collectives, on_device(): start_total = lax.psum(jnp.sum(start * start), 'op')  17.2 us
    psum x1, blocking collectives, on_device(): energy = lax.psum(jnp.sum(vector * image), 'op')  17 us
    dot_general x5, matrix products, apply_field(): jnp.einsum('kij,kjl->kil', middle, right_block, preferred_element_type=jn...  14.7 us
    dot_general x3, matrix products, compose(): jnp.einsum('kij,kjl->kil', earlier, later, precision=lax.Precision.HIGHEST)  9.25 us
  transfers between devices with their start and end apart: 11, of which 1 were waited for; matrix products, arithmetic and copies ran while one was open for 15% of the time, Pallas kernels for 0%

commit v1 on v0

v1 whole, which is shorter than its diff:
```python
import functools

import jax
import jax.numpy as jnp
from jax import lax
from jax.experimental import pallas as pl
from jax.experimental.pallas import tpu as pltpu
from jax.sharding import PartitionSpec as P

DAVIDSON = 4
STEPS = DAVIDSON + 1
ROUNDS = DAVIDSON + 2
CHUNKS = 2

epsilon = 1e-06

MESH = pl.DeviceIdType.MESH
f32 = jnp.float32
bf16 = jnp.bfloat16


def mm(a, b):
    return jnp.dot(a, b, preferred_element_type=f32)


def split(x):
    high = x.astype(bf16)
    return high, (x - high.astype(f32)).astype(bf16)


def folded(x):
    rows, width = x.shape
    x = jnp.sum(x.reshape(rows // 8, 8, width), axis=0)
    acc = x[:, :128]
    for start in range(128, width, 128):
        acc = acc + x[:, start : start + 128]
    return jnp.sum(acc, axis=0, keepdims=True)


def kernel(
    n_seg, n_op,
    theta_ref, edge_ref, transfer_ref, right_ref, coupling_ref, rows_ref, cols_ref,
    vec_out, left_out, energy_out, first_out,
    field, prev, foll, next_coupling, lifted_coupling, arrived, left_wide, right_blk, middle,
    vec, img, app, sums, level,
    field_send, prev_recv, foll_recv, t_send, t_recv, c_send, c_recv, sum_send, sum_recv,
):
    seg = lax.axis_index("seg")
    me = lax.axis_index("op")
    size = theta_ref.shape[-1]
    width = size // CHUNKS
    has_prev = me > 0
    has_next = me < n_op - 1

    barrier = pltpu.get_barrier_semaphore()
    for d in range(1, n_seg):
        pl.semaphore_signal(
            barrier, inc=1, device_id=(lax.rem(seg + d, n_seg), me), device_id_type=MESH
        )
    for d in range(1, n_op):
        pl.semaphore_signal(
            barrier, inc=1, device_id=(seg, lax.rem(me + d, n_op)), device_id_type=MESH
        )

    live_rows = lax.broadcasted_iota(jnp.int32, (size, width), 0) < rows_ref[0]

    def live(c):
        cols = lax.broadcasted_iota(jnp.int32, (size, width), 1) + c * width
        return live_rows & (cols < cols_ref[0])

    for c in range(CHUNKS):
        cs = pl.ds(c * width, width)
        field[0, c] = jnp.where(live(c), theta_ref[0, 0, :, cs].astype(f32), 0.0).astype(bf16)

    pl.semaphore_wait(barrier, n_seg + n_op - 2)

    def t_copy(d):
        return pltpu.make_async_remote_copy(
            src_ref=transfer_ref.at[0, 0], dst_ref=arrived.at[seg],
            send_sem=t_send.at[d], recv_sem=t_recv.at[seg],
            device_id=(seg + d, me), device_id_type=MESH,
        )

    for d in range(1, n_seg):
        @pl.when(seg + d < n_seg)
        def _():
            t_copy(d).start()

    def up_copy(step, c):
        return pltpu.make_async_remote_copy(
            src_ref=field.at[step, c], dst_ref=prev.at[step, c],
            send_sem=field_send.at[step, 0, c], recv_sem=prev_recv.at[step, c],
            device_id=(seg, me + 1), device_id_type=MESH,
        )

    def down_copy(step, c):
        return pltpu.make_async_remote_copy(
            src_ref=field.at[step, c], dst_ref=foll.at[step, c],
            send_sem=field_send.at[step, 1, c], recv_sem=foll_recv.at[step, c],
            device_id=(seg, me - 1), device_id_type=MESH,
        )

    def send_field(step, c):
        @pl.when(has_next)
        def _():
            up_copy(step, c).start()

        @pl.when(has_prev)
        def _():
            down_copy(step, c).start()

    def take_field(step, c):
        @pl.when(has_prev)
        def _():
            up_copy(step, c).wait_recv()

        @pl.when(has_next)
        def _():
            down_copy(step, c).wait_recv()

    def settle_field(step, c):
        @pl.when(has_next)
        def _():
            up_copy(step, c).wait_send()

        @pl.when(has_prev)
        def _():
            down_copy(step, c).wait_send()

    def coupling_copy():
        return pltpu.make_async_remote_copy(
            src_ref=coupling_ref.at[0, 0], dst_ref=next_coupling,
            send_sem=c_send, recv_sem=c_recv,
            device_id=(seg, me - 1), device_id_type=MESH,
        )

    for c in range(CHUNKS):
        send_field(0, c)

    @pl.when(has_prev)
    def _():
        coupling_copy().start()

    def sum_copy(rnd, d):
        return pltpu.make_async_remote_copy(
            src_ref=sums.at[rnd, me], dst_ref=sums.at[rnd, me],
            send_sem=sum_send.at[rnd, d], recv_sem=sum_recv.at[rnd, me],
            device_id=(seg, lax.rem(me + d, n_op)), device_id_type=MESH,
        )

    def sum_start(rnd, parts):
        row = lax.broadcasted_iota(jnp.int32, (8, 128), 0)
        tile = jnp.zeros((8, 128), f32)
        for i, part in enumerate(parts):
            tile = jnp.where(row == i, part, tile)
        sums[rnd, me] = tile
        for d in range(1, n_op):
            sum_copy(rnd, d).start()

    def sum_finish(rnd, count):
        for d in range(1, n_op):
            source = lax.rem(me + d, n_op)
            pltpu.make_async_remote_copy(
                src_ref=sums.at[rnd, source], dst_ref=sums.at[rnd, source],
                send_sem=sum_send.at[rnd, d], recv_sem=sum_recv.at[rnd, source],
                device_id=(seg, source), device_id_type=MESH,
            ).wait_recv()
        total = sums[rnd, 0]
        for p in range(1, n_op):
            total = total + sums[rnd, p]
        total = jnp.sum(total, axis=1, keepdims=True)
        return [total[i : i + 1] for i in range(count)]

    def sum_settle(rnd):
        for d in range(1, n_op):
            sum_copy(rnd, d).wait_send()

    start_part = jnp.zeros((1, 128), f32)
    for c in range(CHUNKS):
        wide = field[0, c].astype(f32)
        start_part += folded(wide * wide)
    sum_start(0, [start_part])

    right = right_ref[0, 0].astype(f32)
    right_blk[...] = (0.5 * (right + right.T)).astype(bf16)

    @pl.when(jnp.logical_not(has_prev))
    def _():
        prev[...] = jnp.zeros_like(prev)

    @pl.when(jnp.logical_not(has_next))
    def _():
        foll[...] = jnp.zeros_like(foll)
        lifted_coupling[...] = jnp.zeros_like(lifted_coupling)

    edge = edge_ref[0].astype(f32)
    left_wide[...] = 0.5 * (edge + edge.T)

    (start_total,) = sum_finish(0, 1)
    start_norm = jnp.sqrt(start_total + epsilon)

    @pl.when(has_next)
    def _():
        down = coupling_copy()
        down.wait_recv()
        lifted_coupling[...] = next_coupling[...].astype(f32).T.astype(bf16)

    for c in range(CHUNKS):
        vec[c] = field[0, c].astype(f32) / start_norm
        take_field(0, c)
        before = (prev[0, c].astype(f32) / start_norm).astype(bf16)
        after = (foll[0, c].astype(f32) / start_norm).astype(bf16)
        app[c] = mm(coupling_ref[0, 0], before) + mm(lifted_coupling[...], after)

    for j in range(n_seg - 1):
        @pl.when(j < seg)
        def _():
            pltpu.make_async_remote_copy(
                src_ref=transfer_ref.at[0, 0], dst_ref=arrived.at[j],
                send_sem=t_send.at[0], recv_sem=t_recv.at[j],
                device_id=(seg - 1, me), device_id_type=MESH,
            ).wait_recv()
            step = arrived[j]
            flipped = step.astype(f32).T.astype(bf16)
            high, low = split(left_wide[...])
            high, low = split(mm(high, step) + mm(low, step))
            left_wide[...] = mm(flipped, high) + mm(flipped, low)

    left_out[0, 0] = left_wide[...].astype(bf16)

    for c in range(CHUNKS):
        cs = pl.ds(c * width, width)
        middle[:, cs] = mm(left_out[0, 0], vec[c].astype(bf16)).astype(bf16)
    energy_part = jnp.zeros((1, 128), f32)
    for c in range(CHUNKS):
        cs = pl.ds(c * width, width)
        image = jnp.where(live(c), mm(middle[...], right_blk[:, cs]) + app[c], 0.0)
        img[c] = image
        energy_part += folded(vec[c] * image)
    sum_start(1, [energy_part])
    (energy,) = sum_finish(1, 1)
    first_out[0] = energy[0, 0]

    for c in range(CHUNKS):
        field[1, c] = (img[c] - energy * vec[c]).astype(bf16)
        send_field(1, c)
    level[...] = jnp.broadcast_to(energy, level.shape)

    def sweep(step, carry):
        energy = level[0:1, 0:1]
        norm_part = jnp.zeros((1, 128), f32)
        cross_part = jnp.zeros((1, 128), f32)
        curv_part = jnp.zeros((1, 128), f32)
        for c in range(CHUNKS):
            cs = pl.ds(c * width, width)
            middle[:, cs] = mm(left_out[0, 0], field[step, c]).astype(bf16)
        for c in range(CHUNKS):
            cs = pl.ds(c * width, width)
            app[c] = mm(middle[...], right_blk[:, cs])
            wide = field[step, c].astype(f32)
            norm_part += folded(wide * wide)
            cross_part += folded(img[c] * wide)
        for c in range(CHUNKS):
            take_field(step, c)
            applied = app[c] + mm(coupling_ref[0, 0], prev[step, c])
            applied = applied + mm(lifted_coupling[...], foll[step, c])
            applied = jnp.where(live(c), applied, 0.0)
            app[c] = applied
            curv_part += folded(applied * field[step, c].astype(f32))
        sum_start(step + 1, [norm_part, cross_part, curv_part])
        corr_norm, cross_term, curv_term = sum_finish(step + 1, 3)

        scale_norm = jnp.sqrt(corr_norm + epsilon)
        offdiag = cross_term / scale_norm
        diag_value = curv_term / (corr_norm + epsilon)
        half_gap = (diag_value - energy) / 2
        lowest = (energy + diag_value) / 2 - jnp.sqrt(half_gap * half_gap + offdiag * offdiag)
        rotation = lowest - energy
        radius = jnp.sqrt(offdiag * offdiag + rotation * rotation + epsilon)
        keep = offdiag / radius
        turn = rotation / scale_norm / radius
        level[...] = jnp.broadcast_to(lowest, level.shape)

        @pl.when(step < DAVIDSON)
        def _():
            for c in range(CHUNKS):
                vector = keep * vec[c] + turn * field[step, c].astype(f32)
                image = keep * img[c] + turn * app[c]
                field[step + 1, c] = (image - lowest * vector).astype(bf16)
                send_field(step + 1, c)
                vec[c] = vector
                img[c] = image

        @pl.when(step == DAVIDSON)
        def _():
            for c in range(CHUNKS):
                cs = pl.ds(c * width, width)
                vec_out[0, 0, :, cs] = keep * vec[c] + turn * field[step, c].astype(f32)

        for c in range(CHUNKS):
            settle_field(step, c)
        sum_settle(step + 1)
        return carry

    lax.fori_loop(1, STEPS, sweep, 0)
    energy_out[0] = level[0:1, 0:1][0, 0]

    for d in range(1, n_seg):
        @pl.when(seg + d < n_seg)
        def _():
            t_copy(d).wait_send()
    for c in range(CHUNKS):
        settle_field(0, c)

    @pl.when(has_prev)
    def _():
        coupling_copy().wait_send()

    sum_settle(0)
    sum_settle(1)


def on_device(n_seg, n_op, *arrays):
    size = arrays[0].shape[-1]
    width = size // CHUNKS
    vmem = pl.BlockSpec(memory_space=pltpu.VMEM)
    smem = pl.BlockSpec(memory_space=pltpu.SMEM)
    dma = pltpu.SemaphoreType.DMA
    fields = (STEPS, CHUNKS, size, width)
    return pl.pallas_call(
        functools.partial(kernel, n_seg, n_op),
        out_shape=(
            jax.ShapeDtypeStruct((1, 1, size, size), f32),
            jax.ShapeDtypeStruct((1, 1, size, size), bf16),
            jax.ShapeDtypeStruct((1,), f32),
            jax.ShapeDtypeStruct((1,), f32),
        ),
        in_specs=[vmem] * 5 + [smem] * 2,
        out_specs=(vmem, vmem, smem, smem),
        scratch_shapes=[
            pltpu.VMEM(fields, bf16),
            pltpu.VMEM(fields, bf16),
            pltpu.VMEM(fields, bf16),
            pltpu.VMEM((size, size), bf16),
            pltpu.VMEM((size, size), bf16),
            pltpu.VMEM((n_seg - 1, size, size), bf16),
            pltpu.VMEM((size, size), f32),
            pltpu.VMEM((size, size), bf16),
            pltpu.VMEM((size, size), bf16),
            pltpu.VMEM((CHUNKS, size, width), f32),
            pltpu.VMEM((CHUNKS, size, width), f32),
            pltpu.VMEM((CHUNKS, size, width), f32),
            pltpu.VMEM((ROUNDS, n_op, 8, 128), f32),
            pltpu.VMEM((8, 128), f32),
            dma((STEPS, 2, CHUNKS)),
            dma((STEPS, CHUNKS)),
            dma((STEPS, CHUNKS)),
            dma((n_seg,)),
            dma((n_seg,)),
            dma,
            dma,
            dma((ROUNDS, n_op)),
            dma((ROUNDS, n_op)),
        ],
        compiler_params=pltpu.CompilerParams(
            collective_id=0, has_side_effects=True, vmem_limit_bytes=48 * 1024 * 1024
        ),
        cost_estimate=pl.CostEstimate(
            flops=2 * 30 * size**3, bytes_accessed=8 * size * size * 2, transcendentals=0
        ),
        name="segment_solve",
    )(*arrays)


def solution(mesh):
    placed = (
        P("seg", "op", None, None),
        P("op", None, None),
        P("seg", "op", None, None),
        P("seg", "op", None, None),
        P("seg", "op", None, None),
        P("op"),
        P("op"),
    )
    return jax.shard_map(
        functools.partial(on_device, mesh.shape["seg"], mesh.shape["op"]),
        mesh=mesh,
        in_specs=placed,
        out_specs=(P("seg", "op", None, None), P("seg", "op", None, None), P("seg"), P("seg")),
        check_vma=False,
    )
```

time: 264 us -> 99 us (0.38); the launches traced: 260 us -> 98.4 us
  blocking collectives: 111 us -> 0 us
  Pallas kernels: 0 us -> 86 us
  matrix products: 54 us -> 0 us
  starting transfers between devices: 23.9 us -> 0 us
  between operations: 27.3 us -> 5.45 us
  other arithmetic: 21.3 us -> 0 us
  waiting for transfers between devices: 19.9 us -> 0 us
  local copies, waits for them, and re-layouts: 3 us -> 6.96 us
    psum x6 -> x0, blocking collectives: 111 us -> none  [the longest x4 76.8 us: on_device(): lax.psum((jnp.sum(corr_wide * corr_wide), jnp.sum(image * corr_wide)), 'op')]
    pallas_call x0 -> x1, Pallas kernels: none -> 86 us  [on_device(): pl.pallas_call(functools.partial(kernel, n_seg, n_op), out_shape=(jax.Sha...]
    dot_general x20 -> x0, matrix products: 54 us -> none  [the longest x5 17.7 us: apply_field(): jnp.einsum('kij,kjl->kil', coupling_blk, previous, preferred_element_type...]
    ppermute x10 -> x0, starting transfers between devices: 23.9 us -> none  [from_behind(): return lax.ppermute(block, axis, route)]
    all_gather x1 -> x0, waiting for transfers between devices: 19.9 us -> none  [carried_in(): pieces = lax.all_gather(value, axis)]
    convert_element_type x7 -> x0, other arithmetic: 11.4 us -> none  [the longest x3 6.72 us: on_device(): correction = residual.astype(jnp.bfloat16)]
    unnamed x19 -> x12, local copies, waits for them, and re-layouts: 0.26 us -> 6.96 us
    reduce_sum x2 -> x0, other arithmetic: 5.22 us -> none  [the longest x1 3.29 us: on_device(): jnp.sum(corr_wide * corr_wide)]
  transfers between devices with their start and end apart: 11 -> 0, of which waited for: 1 -> 0; matrix products, arithmetic and copies ran while one was open for 15% -> 0% of each run, Pallas kernels for 0% -> 0%
where the time goes in v1:
time: 99 us; the launch traced here: 98.4 us
  Pallas kernels  86 us (87%)
  local copies, waits for them, and re-layouts  6.96 us (7%)
  between operations  5.45 us (6%)
    pallas_call x1, Pallas kernels, on_device(): pl.pallas_call(functools.partial(kernel, n_seg, n_op), out_shape=(jax.Sha...  86 us
    unnamed x12, local copies, waits for them, and re-layouts  6.96 us

profile of v1, /device:TPU:6, one launch (start us, length us, event | category | flops | bytes accessed | tf_op | source)
XLA Modules:
  0.0 98.4 jit_solution(14450761528640252891)
XLA Ops:
  1.9 0.0 copy-start
  1.9 1.0 %copy-done = bf16[1,1,512,512]{3,2,1,0:T(8,128)(2,1)S(1)} copy-done((bf16[1,1,512,512]{3,2,1,0:T(8,128)(2,1)S(1)}, bf16[1,1,512,512]{3,2,1,0:T(8,128)(2,1)}, u32[]{:S(2)}) %copy-start) | copy-done | bytes 524312
  3.0 0.0 copy-start.1
  3.0 1.0 %copy-done.1 = bf16[1,512,512]{2,1,0:T(8,128)(2,1)S(1)} copy-done((bf16[1,512,512]{2,1,0:T(8,128)(2,1)S(1)}, bf16[1,512,512]{2,1,0:T(8,128)(2,1)}, u32[]{:S(2)}) %copy-start.1) | copy-done | bytes 524312
  4.0 0.0 copy-start.2
  4.0 1.0 %copy-done.2 = bf16[1,1,512,512]{3,2,1,0:T(8,128)(2,1)S(1)} copy-done((bf16[1,1,512,512]{3,2,1,0:T(8,128)(2,1)S(1)}, bf16[1,1,512,512]{3,2,1,0:T(8,128)(2,1)}, u32[]{:S(2)}) %copy-start.2) | copy-done | bytes 524312
  5.0 0.0 copy-start.3
  5.1 1.0 %copy-done.3 = bf16[1,1,512,512]{3,2,1,0:T(8,128)(2,1)S(1)} copy-done((bf16[1,1,512,512]{3,2,1,0:T(8,128)(2,1)S(1)}, bf16[1,1,512,512]{3,2,1,0:T(8,128)(2,1)}, u32[]{:S(2)}) %copy-start.3) | copy-done | bytes 524312
  6.1 0.0 copy-start.4
  6.1 1.0 %copy-done.4 = bf16[1,1,512,512]{3,2,1,0:T(8,128)(2,1)S(1)} copy-done((bf16[1,1,512,512]{3,2,1,0:T(8,128)(2,1)S(1)}, bf16[1,1,512,512]{3,2,1,0:T(8,128)(2,1)}, u32[]{:S(2)}) %copy-start.4) | copy-done | bytes 524312
  7.1 86.0 %segment_solve.1 = (f32[1,1,512,512]{3,2,1,0:T(8,128)S(1)}, bf16[1,1,512,512]{3,2,1,0:T(8,128)(2,1)S(1)}, f32[1]{0:T(128)}, f32[1]{0:T(128)}) custom-call(bf16[1,1,512,512]{3,2,1,0:T(8,128)(2,1)S(1)} %copy-done, bf16[1,512,512]{2,1,0:T(8,128)(2,1)S(1)} %copy-done.1, bf16[1,1,512,512]{3,2,1,0:T(8,128)(2,1)S(1)} %copy-done.2, ...), custom_call_target="tpu_custom_call" | custom-call | flops 8053063680 | bytes 4194304 | tf_op jit(solution)/shard_map/segment_solve/pallas_call | solution.py:330
  93.1 1.0 copy.17
  94.1 0.8 copy.18
Async XLA Ops:
  1.9 1.0 %copy-start = (bf16[1,1,512,512]{3,2,1,0:T(8,128)(2,1)S(1)}, bf16[1,1,512,512]{3,2,1,0:T(8,128)(2,1)}, u32[]{:S(2)}) copy-start(bf16[1,1,512,512]{3,2,1,0:T(8,128)(2,1)} %theta_ref.1) | copy-start | bytes 1572868
  3.0 1.0 %copy-start.1 = (bf16[1,512,512]{2,1,0:T(8,128)(2,1)S(1)}, bf16[1,512,512]{2,1,0:T(8,128)(2,1)}, u32[]{:S(2)}) copy-start(bf16[1,512,512]{2,1,0:T(8,128)(2,1)} %edge_ref.1) | copy-start | bytes 1572868
  4.0 1.0 %copy-start.2 = (bf16[1,1,512,512]{3,2,1,0:T(8,128)(2,1)S(1)}, bf16[1,1,512,512]{3,2,1,0:T(8,128)(2,1)}, u32[]{:S(2)}) copy-start(bf16[1,1,512,512]{3,2,1,0:T(8,128)(2,1)} %transfer_ref.1) | copy-start | bytes 1572868
  5.0 1.0 %copy-start.3 = (bf16[1,1,512,512]{3,2,1,0:T(8,128)(2,1)S(1)}, bf16[1,1,512,512]{3,2,1,0:T(8,128)(2,1)}, u32[]{:S(2)}) copy-start(bf16[1,1,512,512]{3,2,1,0:T(8,128)(2,1)} %right_ref.1) | copy-start | bytes 1572868
  6.1 1.0 %copy-start.4 = (bf16[1,1,512,512]{3,2,1,0:T(8,128)(2,1)S(1)}, bf16[1,1,512,512]{3,2,1,0:T(8,128)(2,1)}, u32[]{:S(2)}) copy-start(bf16[1,1,512,512]{3,2,1,0:T(8,128)(2,1)} %coupling_ref.1) | copy-start | bytes 1572868

commit v2 on v1

--- a/solution.py
+++ b/solution.py
@@ -8,9 +8,11 @@
 from jax.sharding import PartitionSpec as P
 
 DAVIDSON = 4
-STEPS = DAVIDSON + 1
+STEPS = DAVIDSON + 2
 ROUNDS = DAVIDSON + 2
 CHUNKS = 2
+ROW_BLOCKS = 16
+VMEM_LIMIT = 63 * 1024 * 1024
 
 epsilon = 1e-06
 
@@ -28,29 +30,45 @@
     return high, (x - high.astype(f32)).astype(bf16)
 
 
-def folded(x):
+def folded8(x):
     rows, width = x.shape
     x = jnp.sum(x.reshape(rows // 8, 8, width), axis=0)
     acc = x[:, :128]
     for start in range(128, width, 128):
         acc = acc + x[:, start : start + 128]
-    return jnp.sum(acc, axis=0, keepdims=True)
+    return acc
+
+
+def folded(x):
+    return jnp.sum(folded8(x), axis=0, keepdims=True)
 
 
 def kernel(
     n_seg, n_op,
     theta_ref, edge_ref, transfer_ref, right_ref, coupling_ref, rows_ref, cols_ref,
     vec_out, left_out, energy_out, first_out,
-    field, prev, foll, next_coupling, lifted_coupling, arrived, left_wide, right_blk, middle,
-    vec, img, app, sums, level,
-    field_send, prev_recv, foll_recv, t_send, t_recv, c_send, c_recv, sum_send, sum_recv,
+    theta, edge, right, coupling, own_step, first_left, flipped,
+    field, prev, foll, next_coupling, lifted_coupling, arrived, left_wide, right_blk,
+    middle, middle_low, low, vec, img, him, app, sums, level,
+    load_sem, l_send, l_recv, field_send, prev_recv, foll_recv, t_send, t_recv, c_send, c_recv, sum_send, sum_recv,
 ):
     seg = lax.axis_index("seg")
     me = lax.axis_index("op")
     size = theta_ref.shape[-1]
     width = size // CHUNKS
+    square = n_seg == 4
     has_prev = me > 0
     has_next = me < n_op - 1
+
+    loads = [
+        pltpu.make_async_copy(ref, held, load_sem.at[i])
+        for i, (ref, held) in enumerate((
+            (theta_ref.at[0, 0], theta), (coupling_ref.at[0, 0], coupling),
+            (edge_ref.at[0], edge), (transfer_ref.at[0, 0], own_step), (right_ref.at[0, 0], right),
+        ))
+    ]
+    for load in loads:
+        load.start()
 
     barrier = pltpu.get_barrier_semaphore()
     for d in range(1, n_seg):
@@ -68,9 +86,10 @@
         cols = lax.broadcasted_iota(jnp.int32, (size, width), 1) + c * width
         return live_rows & (cols < cols_ref[0])
 
+    loads[0].wait()
     for c in range(CHUNKS):
         cs = pl.ds(c * width, width)
-        field[0, c] = jnp.where(live(c), theta_ref[0, 0, :, cs].astype(f32), 0.0).astype(bf16)
+        field[0, c] = jnp.where(live(c), theta[:, cs].astype(f32), 0.0).astype(bf16)
 
     pl.semaphore_wait(barrier, n_seg + n_op - 2)
 
@@ -81,10 +100,49 @@
             device_id=(seg + d, me), device_id_type=MESH,
         )
 
-    for d in range(1, n_seg):
-        @pl.when(seg + d < n_seg)
-        def _():
-            t_copy(d).start()
+    quarter = size // 4
+
+    def rows_of(i):
+        return pl.ds(i * quarter, quarter)
+
+    def l_copy(i, path, target):
+        part = first_left.at[rows_of(i), pl.ds(i * quarter, size - i * quarter)]
+        return pltpu.make_async_remote_copy(
+            src_ref=part, dst_ref=part, send_sem=l_send.at[path, i], recv_sem=l_recv.at[i],
+            device_id=(target, me), device_id_type=MESH,
+        )
+
+    def step_copy(i, sem, target, forwarded):
+        part = arrived.at[1, rows_of(i)]
+        return pltpu.make_async_remote_copy(
+            src_ref=part if forwarded else transfer_ref.at[0, 0, rows_of(i)], dst_ref=part,
+            send_sem=t_send.at[sem], recv_sem=t_recv.at[i],
+            device_id=(target, me), device_id_type=MESH,
+        )
+
+    def last_copy():
+        return pltpu.make_async_remote_copy(
+            src_ref=transfer_ref.at[0, 0], dst_ref=arrived.at[2],
+            send_sem=t_send.at[4], recv_sem=t_recv.at[4],
+            device_id=(3, me), device_id_type=MESH,
+        )
+
+    if square:
+        @pl.when(seg == 1)
+        def _():
+            for i in (1, 2, 3):
+                step_copy(i, i, 3, False).start()
+            step_copy(0, 4, 0, False).start()
+            step_copy(0, 0, 3, False).start()
+
+        @pl.when(seg == 2)
+        def _():
+            last_copy().start()
+    else:
+        for d in range(1, n_seg):
+            @pl.when(seg + d < n_seg)
+            def _():
+                t_copy(d).start()
 
     def up_copy(step, c):
         return pltpu.make_async_remote_copy(
@@ -181,8 +239,55 @@
         start_part += folded(wide * wide)
     sum_start(0, [start_part])
 
-    right = right_ref[0, 0].astype(f32)
-    right_blk[...] = (0.5 * (right + right.T)).astype(bf16)
+    for load in loads[1:]:
+        load.wait()
+    edge_wide = edge[...].astype(f32)
+    left_wide[...] = 0.5 * (edge_wide + edge_wide.T)
+
+    def flip(step):
+        flipped[...] = step.astype(f32).T.astype(bf16)
+
+    def advance(left, step):
+        if left.dtype == bf16:
+            image = mm(left, step)
+        else:
+            high, rest = split(left)
+            image = mm(high, step) + mm(rest, step)
+        high, rest = split(image)
+        return mm(flipped[...], high) + mm(flipped[...], rest)
+
+    def mirror():
+        for i in range(4):
+            for j in range(i + 1, 4):
+                block = first_left[rows_of(i), rows_of(j)].astype(f32)
+                first_left[rows_of(j), rows_of(i)] = block.T.astype(bf16)
+
+    if square:
+        @pl.when(seg == 0)
+        def _():
+            flip(own_step[...])
+            first_left[...] = advance(left_wide[...], own_step[...]).astype(bf16)
+            for i in range(4):
+                l_copy(i, 0, 1).start()
+                l_copy(i, 1, 2).start()
+            step_copy(0, 0, 2, True).wait_recv()
+            step_copy(0, 0, 2, True).start()
+
+        for here, turns in ((1, (0, 3)), (2, (1, 2))):
+            @pl.when(seg == here)
+            def _():
+                for i in turns:
+                    l_copy(i, 0, 3).wait_recv()
+                    l_copy(i, 0, 3).start()
+
+        @pl.when(seg == 3)
+        def _():
+            for i in (1, 2, 3):
+                step_copy(i, i, 2, True).wait_recv()
+                step_copy(i, i, 2, True).start()
+
+    right_wide = right[...].astype(f32)
+    right_blk[...] = (0.5 * (right_wide + right_wide.T)).astype(bf16)
 
     @pl.when(jnp.logical_not(has_prev))
     def _():
@@ -192,9 +297,6 @@
     def _():
         foll[...] = jnp.zeros_like(foll)
         lifted_coupling[...] = jnp.zeros_like(lifted_coupling)
-
-    edge = edge_ref[0].astype(f32)
-    left_wide[...] = 0.5 * (edge + edge.T)
 
     (start_total,) = sum_finish(0, 1)
     start_norm = jnp.sqrt(start_total + epsilon)
@@ -210,66 +312,131 @@
         take_field(0, c)
         before = (prev[0, c].astype(f32) / start_norm).astype(bf16)
         after = (foll[0, c].astype(f32) / start_norm).astype(bf16)
-        app[c] = mm(coupling_ref[0, 0], before) + mm(lifted_coupling[...], after)
-
-    for j in range(n_seg - 1):
-        @pl.when(j < seg)
-        def _():
-            pltpu.make_async_remote_copy(
-                src_ref=transfer_ref.at[0, 0], dst_ref=arrived.at[j],
-                send_sem=t_send.at[0], recv_sem=t_recv.at[j],
-                device_id=(seg - 1, me), device_id_type=MESH,
-            ).wait_recv()
-            step = arrived[j]
-            flipped = step.astype(f32).T.astype(bf16)
-            high, low = split(left_wide[...])
-            high, low = split(mm(high, step) + mm(low, step))
-            left_wide[...] = mm(flipped, high) + mm(flipped, low)
+        app[c] = mm(coupling[...], before) + mm(lifted_coupling[...], after)
+
+    if square:
+        @pl.when(seg == 1)
+        def _():
+            for i in (1, 2):
+                l_copy(i, 0, 3).wait_recv()
+            mirror()
+            left_wide[...] = first_left[...].astype(f32)
+
+        @pl.when(seg == 2)
+        def _():
+            for i in range(4):
+                step_copy(i, 0, 3, True).wait_recv()
+            flip(arrived[1])
+            for i in (0, 3):
+                l_copy(i, 0, 3).wait_recv()
+            mirror()
+            left_wide[...] = advance(first_left[...], arrived[1])
+
+        @pl.when(seg == 3)
+        def _():
+            step_copy(0, 0, 2, True).wait_recv()
+            flip(arrived[1])
+            for i in range(4):
+                l_copy(i, 0, 3).wait_recv()
+            mirror()
+            left_wide[...] = advance(first_left[...], arrived[1])
+            last_copy().wait_recv()
+            flip(arrived[2])
+            left_wide[...] = advance(left_wide[...], arrived[2])
+    else:
+        for j in range(n_seg - 1):
+            @pl.when(j < seg)
+            def _():
+                pltpu.make_async_remote_copy(
+                    src_ref=transfer_ref.at[0, 0], dst_ref=arrived.at[j],
+                    send_sem=t_send.at[0], recv_sem=t_recv.at[j],
+                    device_id=(seg - 1, me), device_id_type=MESH,
+                ).wait_recv()
+                flip(arrived[j])
+                left_wide[...] = advance(left_wide[...], arrived[j])
 
     left_out[0, 0] = left_wide[...].astype(bf16)
 
     for c in range(CHUNKS):
         cs = pl.ds(c * width, width)
         middle[:, cs] = mm(left_out[0, 0], vec[c].astype(bf16)).astype(bf16)
-    energy_part = jnp.zeros((1, 128), f32)
+    block = size // ROW_BLOCKS
+    zero = jnp.zeros((1, 128), f32)
+
+    def passes(body, sums_count):
+        def one(i, parts):
+            found = body(pl.ds(pl.multiple_of(i * block, block), block))
+            return tuple(p + folded8(x) for p, x in zip(parts, found))
+
+        start = tuple(jnp.zeros((8, 128), f32) for _ in range(sums_count))
+        parts = lax.fori_loop(0, ROW_BLOCKS, one, start)
+        return [jnp.sum(p, axis=0, keepdims=True) for p in parts]
+
+    def live_block(c, rows):
+        row = lax.broadcasted_iota(jnp.int32, (block, width), 0) + rows.start
+        col = lax.broadcasted_iota(jnp.int32, (block, width), 1) + c * width
+        return (row < rows_ref[0]) & (col < cols_ref[0])
+
+    def diagonal(step):
+        for c in range(CHUNKS):
+            cs = pl.ds(c * width, width)
+            high, rest = split(mm(left_out[0, 0], field[step, c]) + mm(left_out[0, 0], low[c]))
+            middle[:, cs] = high
+            middle_low[:, cs] = rest
+        for c in range(CHUNKS):
+            cs = pl.ds(c * width, width)
+            app[c] = mm(middle[...], right_blk[:, cs]) + mm(middle_low[...], right_blk[:, cs])
+
+    def hop(step, c):
+        take_field(step, c)
+        app[c] += mm(coupling[...], prev[step, c]) + mm(lifted_coupling[...], foll[step, c])
+
+    energy_part = zero
     for c in range(CHUNKS):
         cs = pl.ds(c * width, width)
-        image = jnp.where(live(c), mm(middle[...], right_blk[:, cs]) + app[c], 0.0)
-        img[c] = image
-        energy_part += folded(vec[c] * image)
-    sum_start(1, [energy_part])
+        app[c] += mm(middle[...], right_blk[:, cs])
+
+        def first_pass(rows):
+            image = jnp.where(live_block(c, rows), app[c, rows], 0.0)
+            img[c, rows] = image
+            high, rest = split(image)
+            field[1, c, rows] = high
+            low[c, rows] = rest
+            return (vec[c, rows] * image,)
+
+        (part,) = passes(first_pass, 1)
+        energy_part += part
+        if c == CHUNKS - 1:
+            sum_start(1, [energy_part])
+        send_field(1, c)
+    diagonal(1)
     (energy,) = sum_finish(1, 1)
     first_out[0] = energy[0, 0]
-
-    for c in range(CHUNKS):
-        field[1, c] = (img[c] - energy * vec[c]).astype(bf16)
-        send_field(1, c)
     level[...] = jnp.broadcast_to(energy, level.shape)
 
-    def sweep(step, carry):
+    totals = [zero, zero, zero]
+    for c in range(CHUNKS):
+        hop(1, c)
+
+        def second_pass(rows):
+            twice = jnp.where(live_block(c, rows), app[c, rows], 0.0)
+            him[c, rows] = twice
+            image = img[c, rows]
+            corr = image - energy * vec[c, rows]
+            applied = twice - energy * image
+            high, rest = split(applied)
+            field[2, c, rows] = high
+            low[c, rows] = rest
+            return corr * corr, image * corr, corr * applied
+
+        totals = [t + p for t, p in zip(totals, passes(second_pass, 3))]
+        if c == CHUNKS - 1:
+            sum_start(2, totals)
+        send_field(2, c)
+
+    def rotate(step):
         energy = level[0:1, 0:1]
-        norm_part = jnp.zeros((1, 128), f32)
-        cross_part = jnp.zeros((1, 128), f32)
-        curv_part = jnp.zeros((1, 128), f32)
-        for c in range(CHUNKS):
-            cs = pl.ds(c * width, width)
-            middle[:, cs] = mm(left_out[0, 0], field[step, c]).astype(bf16)
-        for c in range(CHUNKS):
-            cs = pl.ds(c * width, width)
-            app[c] = mm(middle[...], right_blk[:, cs])
-            wide = field[step, c].astype(f32)
-            norm_part += folded(wide * wide)
-            cross_part += folded(img[c] * wide)
-        for c in range(CHUNKS):
-            take_field(step, c)
-            applied = app[c] + mm(coupling_ref[0, 0], prev[step, c])
-            applied = applied + mm(lifted_coupling[...], foll[step, c])
-            applied = jnp.where(live(c), applied, 0.0)
-            app[c] = applied
-            curv_part += folded(applied * field[step, c].astype(f32))
-        sum_start(step + 1, [norm_part, cross_part, curv_part])
         corr_norm, cross_term, curv_term = sum_finish(step + 1, 3)
-
         scale_norm = jnp.sqrt(corr_norm + epsilon)
         offdiag = cross_term / scale_norm
         diag_value = curv_term / (corr_norm + epsilon)
@@ -277,40 +444,97 @@
         lowest = (energy + diag_value) / 2 - jnp.sqrt(half_gap * half_gap + offdiag * offdiag)
         rotation = lowest - energy
         radius = jnp.sqrt(offdiag * offdiag + rotation * rotation + epsilon)
-        keep = offdiag / radius
-        turn = rotation / scale_norm / radius
         level[...] = jnp.broadcast_to(lowest, level.shape)
-
-        @pl.when(step < DAVIDSON)
-        def _():
-            for c in range(CHUNKS):
-                vector = keep * vec[c] + turn * field[step, c].astype(f32)
-                image = keep * img[c] + turn * app[c]
-                field[step + 1, c] = (image - lowest * vector).astype(bf16)
-                send_field(step + 1, c)
-                vec[c] = vector
-                img[c] = image
-
-        @pl.when(step == DAVIDSON)
-        def _():
-            for c in range(CHUNKS):
-                cs = pl.ds(c * width, width)
-                vec_out[0, 0, :, cs] = keep * vec[c] + turn * field[step, c].astype(f32)
-
+        return energy, lowest, offdiag / radius, rotation / scale_norm / radius
+
+    def sweep(step, carry):
+        diagonal(step + 1)
+        energy, lowest, keep, turn = rotate(step)
+        totals = [zero, zero, zero]
         for c in range(CHUNKS):
-            settle_field(step, c)
+            hop(step + 1, c)
+
+            def update(rows):
+                vector, image, twice = vec[c, rows], img[c, rows], him[c, rows]
+                more = jnp.where(live_block(c, rows), app[c, rows], 0.0)
+                corr = image - energy * vector
+                applied = twice - energy * image
+                vector = keep * vector + turn * corr
+                image = keep * image + turn * applied
+                twice = keep * twice + turn * more
+                vec[c, rows] = vector
+                img[c, rows] = image
+                him[c, rows] = twice
+                corr = image - lowest * vector
+                applied = twice - lowest * image
+                high, rest = split(applied)
+                field[step + 2, c, rows] = high
+                low[c, rows] = rest
+                return corr * corr, image * corr, corr * applied
+
+            totals = [t + p for t, p in zip(totals, passes(update, 3))]
+            if c == CHUNKS - 1:
+                sum_start(step + 2, totals)
+
+            @pl.when(step < DAVIDSON - 1)
+            def _():
+                send_field(step + 2, c)
+
+            settle_field(step + 1, c)
         sum_settle(step + 1)
         return carry
 
-    lax.fori_loop(1, STEPS, sweep, 0)
-    energy_out[0] = level[0:1, 0:1][0, 0]
-
-    for d in range(1, n_seg):
-        @pl.when(seg + d < n_seg)
-        def _():
-            t_copy(d).wait_send()
+    lax.fori_loop(1, DAVIDSON, sweep, 0)
+    energy, lowest, keep, turn = rotate(DAVIDSON)
+    for c in range(CHUNKS):
+        cs = pl.ds(c * width, width)
+
+        def last_pass(rows):
+            vector = vec[c, rows]
+            corr = img[c, rows] - energy * vector
+            vec_out[0, 0, rows, cs] = keep * vector + turn * corr
+            return ()
+
+        passes(last_pass, 0)
+    energy_out[0] = lowest[0, 0]
+    sum_settle(DAVIDSON + 1)
+
+    if square:
+        @pl.when(seg == 0)
+        def _():
+            for i in range(4):
+                l_copy(i, 0, 1).wait_send()
+                l_copy(i, 1, 2).wait_send()
+            step_copy(0, 0, 2, True).wait_send()
+
+        @pl.when(seg == 1)
+        def _():
+            for i in range(4):
+                step_copy(i, i, 3, False).wait_send()
+            step_copy(0, 4, 0, False).wait_send()
+
+        for here, turns in ((1, (0, 3)), (2, (1, 2))):
+            @pl.when(seg == here)
+            def _():
+                for i in turns:
+                    l_copy(i, 0, 3).wait_send()
+
+        @pl.when(seg == 2)
+        def _():
+            last_copy().wait_send()
+
+        @pl.when(seg == 3)
+        def _():
+            for i in (1, 2, 3):
+                step_copy(i, i, 2, True).wait_send()
+    else:
+        for d in range(1, n_seg):
+            @pl.when(seg + d < n_seg)
+            def _():
+                t_copy(d).wait_send()
     for c in range(CHUNKS):
         settle_field(0, c)
+        settle_field(1, c)
 
     @pl.when(has_prev)
     def _():
@@ -335,9 +559,16 @@
             jax.ShapeDtypeStruct((1,), f32),
             jax.ShapeDtypeStruct((1,), f32),
         ),
-        in_specs=[vmem] * 5 + [smem] * 2,
+        in_specs=[pl.BlockSpec(memory_space=pltpu.HBM)] * 5 + [smem] * 2,
         out_specs=(vmem, vmem, smem, smem),
         scratch_shapes=[
+            pltpu.VMEM((size, size), bf16),
+            pltpu.VMEM((size, size), bf16),
+            pltpu.VMEM((size, size), bf16),
+            pltpu.VMEM((size, size), bf16),
+            pltpu.VMEM((size, size), bf16),
+            pltpu.VMEM((size, size), bf16),
+            pltpu.VMEM((size, size), bf16),
             pltpu.VMEM(fields, bf16),
             pltpu.VMEM(fields, bf16),
             pltpu.VMEM(fields, bf16),
@@ -347,23 +578,29 @@
             pltpu.VMEM((size, size), f32),
             pltpu.VMEM((size, size), bf16),
             pltpu.VMEM((size, size), bf16),
+            pltpu.VMEM((size, size), bf16),
+            pltpu.VMEM((CHUNKS, size, width), bf16),
+            pltpu.VMEM((CHUNKS, size, width), f32),
             pltpu.VMEM((CHUNKS, size, width), f32),
             pltpu.VMEM((CHUNKS, size, width), f32),
             pltpu.VMEM((CHUNKS, size, width), f32),
             pltpu.VMEM((ROUNDS, n_op, 8, 128), f32),
             pltpu.VMEM((8, 128), f32),
+            dma((5,)),
+            dma((2, 4)),
+            dma((4,)),
             dma((STEPS, 2, CHUNKS)),
             dma((STEPS, CHUNKS)),
             dma((STEPS, CHUNKS)),
-            dma((n_seg,)),
-            dma((n_seg,)),
+            dma((n_seg + 1,)),
+            dma((n_seg + 1,)),
             dma,
             dma,
             dma((ROUNDS, n_op)),
             dma((ROUNDS, n_op)),
         ],
         compiler_params=pltpu.CompilerParams(
-            collective_id=0, has_side_effects=True, vmem_limit_bytes=48 * 1024 * 1024
+            collective_id=0, has_side_effects=True, vmem_limit_bytes=VMEM_LIMIT
         ),
         cost_estimate=pl.CostEstimate(
             flops=2 * 30 * size**3, bytes_accessed=8 * size * size * 2, transcendentals=0

time: 99 us -> 72.8 us (0.74)
  Pallas kernels: 86 us -> 63.7 us
  local copies, waits for them, and re-layouts: 6.96 us -> 3.12 us
    pallas_call x1, Pallas kernels: 86 us -> 63.7 us  [on_device(): pl.pallas_call(functools.partial(kernel, n_seg, n_op), out_shape=(jax.Sha...]
    unnamed x12 -> x4, local copies, waits for them, and re-layouts: 6.96 us -> 3.12 us
where the time goes in v2:
time: 72.8 us; the launch traced here: 72.3 us
  Pallas kernels  63.7 us (88%)
  between operations  5.47 us (8%)
  local copies, waits for them, and re-layouts  3.12 us (4%)
    pallas_call x1, Pallas kernels, on_device(): pl.pallas_call(functools.partial(kernel, n_seg, n_op), out_shape=(jax.Sha...  63.7 us
    unnamed x4, local copies, waits for them, and re-layouts  3.12 us

profile of v2, /device:TPU:6, one launch (start us, length us, event | category | flops | bytes accessed | tf_op | source)
XLA Modules:
  0.0 72.3 jit_solution(13924107771130444569)
XLA Ops:
  1.9 63.7 %segment_solve.1 = (f32[1,1,512,512]{3,2,1,0:T(8,128)}, bf16[1,1,512,512]{3,2,1,0:T(8,128)(2,1)}, f32[1]{0:T(128)}, f32[1]{0:T(128)}) custom-call(bf16[1,1,512,512]{3,2,1,0:T(8,128)(2,1)} %theta_ref.1, bf16[1,512,512]{2,1,0:T(8,128)(2,1)} %edge_ref.1, bf16[1,1,512,512]{3,2,1,0:T(8,128)(2,1)} %transfer_ref.1, bf16[1,1,512,512]{3,2,1,0:T(8,128)(2,1)} %right_ref.1, ...), custom_call_target="tpu_custom_call" | custom-call | flops 8053063680 | bytes 4194304 | tf_op jit(solution)/shard_map/segment_solve/pallas_call | solution.py:554
  65.7 0.0 copy-start
  65.7 2.3 %copy.17 = f32[1,1,512,512]{3,2,1,0:T(8,128)} copy(f32[1,1,512,512]{3,2,1,0:T(8,128)} %get-tuple-element.8) | data formatting | bytes 2097152
  68.0 0.0 copy-done
  68.0 0.8 %copy.18 = bf16[1,1,512,512]{3,2,1,0:T(8,128)(2,1)} copy(bf16[1,1,512,512]{3,2,1,0:T(8,128)(2,1)S(1)} %copy-done) | data formatting | bytes 1048576
Async XLA Ops:
  65.7 2.3 %copy-start = (bf16[1,1,512,512]{3,2,1,0:T(8,128)(2,1)S(1)}, bf16[1,1,512,512]{3,2,1,0:T(8,128)(2,1)}, u32[]{:S(2)}) copy-start(bf16[1,1,512,512]{3,2,1,0:T(8,128)(2,1)} %get-tuple-element.9) | copy-start | bytes 1572868

commit v3 on v2

--- a/solution.py
+++ b/solution.py
@@ -49,7 +49,7 @@
     vec_out, left_out, energy_out, first_out,
     theta, edge, right, coupling, own_step, first_left, flipped,
     field, prev, foll, next_coupling, lifted_coupling, arrived, left_wide, right_blk,
-    middle, middle_low, low, vec, img, him, app, sums, level,
+    middle, vec, img, him, app, sums, level,
     load_sem, l_send, l_recv, field_send, prev_recv, foll_recv, t_send, t_recv, c_send, c_recv, sum_send, sum_recv,
 ):
     seg = lax.axis_index("seg")
@@ -211,7 +211,9 @@
         tile = jnp.zeros((8, 128), f32)
         for i, part in enumerate(parts):
             tile = jnp.where(row == i, part, tile)
-        sums[rnd, me] = tile
+        tile = jnp.sum(tile, axis=1, keepdims=True)
+        lane = lax.broadcasted_iota(jnp.int32, (8, 128), 1)
+        sums[rnd, me] = jnp.sum(jnp.where(lane == row, tile, 0.0), axis=0, keepdims=True)
         for d in range(1, n_op):
             sum_copy(rnd, d).start()
 
@@ -226,8 +228,7 @@
         total = sums[rnd, 0]
         for p in range(1, n_op):
             total = total + sums[rnd, p]
-        total = jnp.sum(total, axis=1, keepdims=True)
-        return [total[i : i + 1] for i in range(count)]
+        return [total[:, i : i + 1] for i in range(count)]
 
     def sum_settle(rnd):
         for d in range(1, n_op):
@@ -380,12 +381,10 @@
     def diagonal(step):
         for c in range(CHUNKS):
             cs = pl.ds(c * width, width)
-            high, rest = split(mm(left_out[0, 0], field[step, c]) + mm(left_out[0, 0], low[c]))
-            middle[:, cs] = high
-            middle_low[:, cs] = rest
+            middle[:, cs] = mm(left_out[0, 0], field[step, c]).astype(bf16)
         for c in range(CHUNKS):
             cs = pl.ds(c * width, width)
-            app[c] = mm(middle[...], right_blk[:, cs]) + mm(middle_low[...], right_blk[:, cs])
+            app[c] = mm(middle[...], right_blk[:, cs])
 
     def hop(step, c):
         take_field(step, c)
@@ -399,9 +398,7 @@
         def first_pass(rows):
             image = jnp.where(live_block(c, rows), app[c, rows], 0.0)
             img[c, rows] = image
-            high, rest = split(image)
-            field[1, c, rows] = high
-            low[c, rows] = rest
+            field[1, c, rows] = image.astype(bf16)
             return (vec[c, rows] * image,)
 
         (part,) = passes(first_pass, 1)
@@ -424,9 +421,7 @@
             image = img[c, rows]
             corr = image - energy * vec[c, rows]
             applied = twice - energy * image
-            high, rest = split(applied)
-            field[2, c, rows] = high
-            low[c, rows] = rest
+            field[2, c, rows] = applied.astype(bf16)
             return corr * corr, image * corr, corr * applied
 
         totals = [t + p for t, p in zip(totals, passes(second_pass, 3))]
@@ -450,6 +445,7 @@
     def sweep(step, carry):
         diagonal(step + 1)
         energy, lowest, keep, turn = rotate(step)
+        stay = keep - turn * energy
         totals = [zero, zero, zero]
         for c in range(CHUNKS):
             hop(step + 1, c)
@@ -457,19 +453,15 @@
             def update(rows):
                 vector, image, twice = vec[c, rows], img[c, rows], him[c, rows]
                 more = jnp.where(live_block(c, rows), app[c, rows], 0.0)
-                corr = image - energy * vector
-                applied = twice - energy * image
-                vector = keep * vector + turn * corr
-                image = keep * image + turn * applied
+                vector = stay * vector + turn * image
+                image = stay * image + turn * twice
                 twice = keep * twice + turn * more
                 vec[c, rows] = vector
                 img[c, rows] = image
                 him[c, rows] = twice
                 corr = image - lowest * vector
                 applied = twice - lowest * image
-                high, rest = split(applied)
-                field[step + 2, c, rows] = high
-                low[c, rows] = rest
+                field[step + 2, c, rows] = applied.astype(bf16)
                 return corr * corr, image * corr, corr * applied
 
             totals = [t + p for t, p in zip(totals, passes(update, 3))]
@@ -578,13 +570,11 @@
             pltpu.VMEM((size, size), f32),
             pltpu.VMEM((size, size), bf16),
             pltpu.VMEM((size, size), bf16),
-            pltpu.VMEM((size, size), bf16),
-            pltpu.VMEM((CHUNKS, size, width), bf16),
             pltpu.VMEM((CHUNKS, size, width), f32),
             pltpu.VMEM((CHUNKS, size, width), f32),
             pltpu.VMEM((CHUNKS, size, width), f32),
             pltpu.VMEM((CHUNKS, size, width), f32),
-            pltpu.VMEM((ROUNDS, n_op, 8, 128), f32),
+            pltpu.VMEM((ROUNDS, n_op, 1, 128), f32),
             pltpu.VMEM((8, 128), f32),
             dma((5,)),
             dma((2, 4)),

time: 72.8 us -> 75.3 us (1.034)
  Pallas kernels: 63.7 us -> 66.5 us
    pallas_call x1, Pallas kernels: 63.7 us -> 66.5 us  [on_device(): pl.pallas_call(functools.partial(kernel, n_seg, n_op), out_shape=(jax.Sha...]
where the time goes in v3:
time: 75.3 us; the launch traced here: 75.1 us
  Pallas kernels  66.5 us (88%)
  between operations  5.47 us (7%)
  local copies, waits for them, and re-layouts  3.12 us (4%)
    pallas_call x1, Pallas kernels, on_device(): pl.pallas_call(functools.partial(kernel, n_seg, n_op), out_shape=(jax.Sha...  66.5 us
    unnamed x4, local copies, waits for them, and re-layouts  3.12 us

profile of v3, /device:TPU:6, one launch (start us, length us, event | category | flops | bytes accessed | tf_op | source)
XLA Modules:
  0.0 75.1 jit_solution(17722052453111237522)
XLA Ops:
  1.9 66.5 %segment_solve.1 = (f32[1,1,512,512]{3,2,1,0:T(8,128)}, bf16[1,1,512,512]{3,2,1,0:T(8,128)(2,1)}, f32[1]{0:T(128)}, f32[1]{0:T(128)}) custom-call(bf16[1,1,512,512]{3,2,1,0:T(8,128)(2,1)} %theta_ref.1, bf16[1,512,512]{2,1,0:T(8,128)(2,1)} %edge_ref.1, bf16[1,1,512,512]{3,2,1,0:T(8,128)(2,1)} %transfer_ref.1, bf16[1,1,512,512]{3,2,1,0:T(8,128)(2,1)} %right_ref.1, ...), custom_call_target="tpu_custom_call" | custom-call | flops 8053063680 | bytes 4194304 | tf_op jit(solution)/shard_map/segment_solve/pallas_call | solution.py:546
  68.4 0.0 copy-start
  68.5 2.3 %copy.17 = f32[1,1,512,512]{3,2,1,0:T(8,128)} copy(f32[1,1,512,512]{3,2,1,0:T(8,128)} %get-tuple-element.8) | data formatting | bytes 2097152
  70.8 0.0 copy-done
  70.8 0.8 %copy.18 = bf16[1,1,512,512]{3,2,1,0:T(8,128)(2,1)} copy(bf16[1,1,512,512]{3,2,1,0:T(8,128)(2,1)S(1)} %copy-done) | data formatting | bytes 1048576
Async XLA Ops:
  68.4 2.3 %copy-start = (bf16[1,1,512,512]{3,2,1,0:T(8,128)(2,1)S(1)}, bf16[1,1,512,512]{3,2,1,0:T(8,128)(2,1)}, u32[]{:S(2)}) copy-start(bf16[1,1,512,512]{3,2,1,0:T(8,128)(2,1)} %get-tuple-element.9) | copy-start | bytes 1572868

commit v4 on v3

--- a/solution.py
+++ b/solution.py
@@ -211,9 +211,7 @@
         tile = jnp.zeros((8, 128), f32)
         for i, part in enumerate(parts):
             tile = jnp.where(row == i, part, tile)
-        tile = jnp.sum(tile, axis=1, keepdims=True)
-        lane = lax.broadcasted_iota(jnp.int32, (8, 128), 1)
-        sums[rnd, me] = jnp.sum(jnp.where(lane == row, tile, 0.0), axis=0, keepdims=True)
+        sums[rnd, me] = tile
         for d in range(1, n_op):
             sum_copy(rnd, d).start()
 
@@ -228,7 +226,8 @@
         total = sums[rnd, 0]
         for p in range(1, n_op):
             total = total + sums[rnd, p]
-        return [total[:, i : i + 1] for i in range(count)]
+        total = jnp.sum(total, axis=1, keepdims=True)
+        return [total[i : i + 1] for i in range(count)]
 
     def sum_settle(rnd):
         for d in range(1, n_op):
@@ -574,7 +573,7 @@
             pltpu.VMEM((CHUNKS, size, width), f32),
             pltpu.VMEM((CHUNKS, size, width), f32),
             pltpu.VMEM((CHUNKS, size, width), f32),
-            pltpu.VMEM((ROUNDS, n_op, 1, 128), f32),
+            pltpu.VMEM((ROUNDS, n_op, 8, 128), f32),
             pltpu.VMEM((8, 128), f32),
             dma((5,)),
             dma((2, 4)),

time: 75.3 us -> 72.3 us (0.960)
  Pallas kernels: 66.5 us -> 63.2 us
    pallas_call x1, Pallas kernels: 66.5 us -> 63.2 us  [on_device(): pl.pallas_call(functools.partial(kernel, n_seg, n_op), out_shape=(jax.Sha...]
where the time goes in v4:
time: 72.3 us; the launch traced here: 71.8 us
  Pallas kernels  63.2 us (87%)
  between operations  5.47 us (8%)
  local copies, waits for them, and re-layouts  3.12 us (4%)
    pallas_call x1, Pallas kernels, on_device(): pl.pallas_call(functools.partial(kernel, n_seg, n_op), out_shape=(jax.Sha...  63.2 us
    unnamed x4, local copies, waits for them, and re-layouts  3.12 us

profile of v4, /device:TPU:6, one launch (start us, length us, event | category | flops | bytes accessed | tf_op | source)
XLA Modules:
  0.0 71.8 jit_solution(12475882634342152473)
XLA Ops:
  1.9 63.2 %segment_solve.1 = (f32[1,1,512,512]{3,2,1,0:T(8,128)}, bf16[1,1,512,512]{3,2,1,0:T(8,128)(2,1)}, f32[1]{0:T(128)}, f32[1]{0:T(128)}) custom-call(bf16[1,1,512,512]{3,2,1,0:T(8,128)(2,1)} %theta_ref.1, bf16[1,512,512]{2,1,0:T(8,128)(2,1)} %edge_ref.1, bf16[1,1,512,512]{3,2,1,0:T(8,128)(2,1)} %transfer_ref.1, bf16[1,1,512,512]{3,2,1,0:T(8,128)(2,1)} %right_ref.1, ...), custom_call_target="tpu_custom_call" | custom-call | flops 8053063680 | bytes 4194304 | tf_op jit(solution)/shard_map/segment_solve/pallas_call | solution.py:545
  65.2 0.0 copy-start
  65.2 2.3 %copy.17 = f32[1,1,512,512]{3,2,1,0:T(8,128)} copy(f32[1,1,512,512]{3,2,1,0:T(8,128)} %get-tuple-element.8) | data formatting | bytes 2097152
  67.5 0.0 copy-done
  67.5 0.8 %copy.18 = bf16[1,1,512,512]{3,2,1,0:T(8,128)(2,1)} copy(bf16[1,1,512,512]{3,2,1,0:T(8,128)(2,1)S(1)} %copy-done) | data formatting | bytes 1048576
Async XLA Ops:
  65.2 2.3 %copy-start = (bf16[1,1,512,512]{3,2,1,0:T(8,128)(2,1)S(1)}, bf16[1,1,512,512]{3,2,1,0:T(8,128)(2,1)}, u32[]{:S(2)}) copy-start(bf16[1,1,512,512]{3,2,1,0:T(8,128)(2,1)} %get-tuple-element.9) | copy-start | bytes 1572868

commit v5 on v4

--- a/solution.py
+++ b/solution.py
@@ -369,7 +369,7 @@
             return tuple(p + folded8(x) for p, x in zip(parts, found))
 
         start = tuple(jnp.zeros((8, 128), f32) for _ in range(sums_count))
-        parts = lax.fori_loop(0, ROW_BLOCKS, one, start)
+        parts = lax.fori_loop(0, ROW_BLOCKS, one, start, unroll=4)
         return [jnp.sum(p, axis=0, keepdims=True) for p in parts]
 
     def live_block(c, rows):

time: 72.3 us -> 70.6 us (0.976)
  Pallas kernels: 63.2 us -> 61.5 us
    pallas_call x1, Pallas kernels: 63.2 us -> 61.5 us  [on_device(): pl.pallas_call(functools.partial(kernel, n_seg, n_op), out_shape=(jax.Sha...]
where the time goes in v5:
time: 70.6 us; the launch traced here: 70.1 us
  Pallas kernels  61.5 us (87%)
  between operations  5.47 us (8%)
  local copies, waits for them, and re-layouts  3.12 us (4%)
    pallas_call x1, Pallas kernels, on_device(): pl.pallas_call(functools.partial(kernel, n_seg, n_op), out_shape=(jax.Sha...  61.5 us
    unnamed x4, local copies, waits for them, and re-layouts  3.12 us

profile of v5, /device:TPU:6, one launch (start us, length us, event | category | flops | bytes accessed | tf_op | source)
XLA Modules:
  0.0 70.1 jit_solution(13787969336583203594)
XLA Ops:
  1.9 61.5 %segment_solve.1 = (f32[1,1,512,512]{3,2,1,0:T(8,128)}, bf16[1,1,512,512]{3,2,1,0:T(8,128)(2,1)}, f32[1]{0:T(128)}, f32[1]{0:T(128)}) custom-call(bf16[1,1,512,512]{3,2,1,0:T(8,128)(2,1)} %theta_ref.1, bf16[1,512,512]{2,1,0:T(8,128)(2,1)} %edge_ref.1, bf16[1,1,512,512]{3,2,1,0:T(8,128)(2,1)} %transfer_ref.1, bf16[1,1,512,512]{3,2,1,0:T(8,128)(2,1)} %right_ref.1, ...), custom_call_target="tpu_custom_call" | custom-call | flops 8053063680 | bytes 4194304 | tf_op jit(solution)/shard_map/segment_solve/pallas_call | solution.py:545
  63.5 0.0 copy-start
  63.5 2.3 %copy.17 = f32[1,1,512,512]{3,2,1,0:T(8,128)} copy(f32[1,1,512,512]{3,2,1,0:T(8,128)} %get-tuple-element.8) | data formatting | bytes 2097152
  65.8 0.0 copy-done
  65.8 0.8 %copy.18 = bf16[1,1,512,512]{3,2,1,0:T(8,128)(2,1)} copy(bf16[1,1,512,512]{3,2,1,0:T(8,128)(2,1)S(1)} %copy-done) | data formatting | bytes 1048576
Async XLA Ops:
  63.5 2.3 %copy-start = (bf16[1,1,512,512]{3,2,1,0:T(8,128)(2,1)S(1)}, bf16[1,1,512,512]{3,2,1,0:T(8,128)(2,1)}, u32[]{:S(2)}) copy-start(bf16[1,1,512,512]{3,2,1,0:T(8,128)(2,1)} %get-tuple-element.9) | copy-start | bytes 1572868
